TPU v7x, 32 devices: a whole 2x2x4 slice. The times are simulated.
32 devices in a mesh: img: 8 (over z, x), ref: 4 (over y, core).
Axes of the slice: x: 2, y: 2, z: 4, core: 2. Of those that a mesh axis runs over, the one named last changes fastest.
Arguments:
- particles: bfloat16 [2048, 4096], P('img'), may hold values from -40 to 40
- projections: bfloat16 [64, 8, 4096], P(('img', 'ref')), may hold values from -6 to 6
- significance: int32 [8, 64], replicated, may hold values from 0 to 1, as said below
- insertion: int32 [64, 8, 2048], P(('img', 'ref')), may hold values from 0 to 4095
Outputs:
- volume: float32 [2, 131072], P(None, ('img', 'ref'))
- log_evidence: float32 [2048], P('img')
Inputs may be any that keep to these rules, and one draw needn't show every extreme that they name: `significance`: runs are blocks o * 2 to o * 2 + 1, o counted over img and ref with img slowest. For each particle block and each run at most one block is significant; particle block q has one in run q * 4; in every draw some particle block has one in every run.
All inputs are finite; a program needn't handle non-finite values.
Results may differ from a plain program's by a relative error of at most 0.00064.
Values may be sent and summed in bfloat16 or wider, within the bound.
A program may use at most 128 MiB of HBM per device.

v0:
```python
import math

import jax
import jax.numpy as jnp
from jax import lax
from jax.sharding import PartitionSpec as P

SIDE = 64
VOX = 4096


SHIFT_X = (0.0, 1.0, -1.0, 0.0, 0.0)
SHIFT_Y = (0.0, 0.0, 0.0, 1.0, -1.0)
NEGATIVE = -1e30


def merged(value, axis, join):
    pieces = jax.tree.map(lambda part: lax.all_gather(part, axis), value)
    head = jax.tree.map(lambda part: part[0], pieces)
    tail = jax.tree.map(lambda part: part[1:], pieces)
    running, _ = lax.scan(lambda running, slab: (join(running, slab), None), head, tail)
    return running


def shifted_images(images, side_cells):
    pixels = images.shape[1] // 2
    positions = jnp.arange(pixels, dtype=jnp.int32)
    freq_x = (positions % side_cells - side_cells // 2).astype(jnp.float32)
    freq_y = (positions // side_cells).astype(jnp.float32)
    shift_x = jnp.array(SHIFT_X, jnp.float32)[:, None]
    shift_y = jnp.array(SHIFT_Y, jnp.float32)[:, None]
    angles = 2.0 * math.pi / side_cells * (shift_x * freq_x[None, :] + shift_y * freq_y[None, :])
    cosine = jnp.cos(angles)
    sine_table = jnp.sin(angles)
    real_part = images[:, None, :pixels].astype(jnp.float32)
    imag_part = images[:, None, pixels:].astype(jnp.float32)
    new_real = real_part * cosine - imag_part * sine_table
    new_imag = real_part * sine_table + imag_part * cosine
    stacked = jnp.concatenate([new_real, new_imag], axis=2).astype(jnp.bfloat16)
    return stacked.reshape(images.shape[0] * len(SHIFT_X), 2 * pixels)


def merge_pairs(left_pair, right_pair):
    joined_top = jnp.maximum(left_pair[0], right_pair[0])
    joined_total = left_pair[1] * jnp.exp(left_pair[0] - joined_top) + right_pair[1] * jnp.exp(
        right_pair[0] - joined_top
    )
    return (joined_top, joined_total)


def insert_slab(weighted, insertion, slab_size):
    blocks_here, block_rows, features = weighted.shape
    pixels = features // 2
    low_count = 64
    high_count = slab_size // low_count
    voxel_ids = insertion.reshape(-1)
    high_ids = voxel_ids // low_count
    low_ids = voxel_ids % low_count
    high_table = (high_ids[None, :] == jnp.arange(high_count, dtype=jnp.int32)[:, None]).astype(
        jnp.float32
    )
    low_table = (low_ids[None, :] == jnp.arange(low_count, dtype=jnp.int32)[:, None]).astype(
        jnp.float32
    )
    coefficients = (
        weighted.reshape(blocks_here * block_rows, 2, pixels).transpose(1, 0, 2).reshape(2, -1)
    )
    scaled_rows = (coefficients[:, None, :] * high_table[None, :, :]).reshape(2 * high_count, -1)
    inserted = jnp.einsum(
        "an,bn->ab",
        scaled_rows,
        low_table,
        precision=lax.Precision.HIGHEST,
        preferred_element_type=jnp.float32,
    )
    return inserted.reshape(2, slab_size)


def per_device(particles, projections, significance, insertion):
    img_count = lax.axis_size("img")
    ref_count = lax.axis_size("ref")
    img_rank = lax.axis_index("img")
    ref_rank = lax.axis_index("ref")
    blocks_here, block_rows, features = projections.shape
    scale_factor = 2.0 / math.sqrt(features)
    shifted = shifted_images(particles, SIDE)
    shift_count = len(SHIFT_X)
    particle_count = particles.shape[0]
    pattern = significance.reshape(img_count, img_count, ref_count, blocks_here)
    pattern_ref = lax.dynamic_index_in_dim(pattern, ref_rank, 2, keepdims=False)
    wanted = lax.dynamic_index_in_dim(pattern_ref, img_rank, 0, keepdims=False)
    requested = lax.dynamic_index_in_dim(pattern_ref, img_rank, 1, keepdims=False)
    live_owner = jnp.sum(wanted, axis=1)
    outgoing = jnp.einsum(
        "qk,kef->qef",
        requested.astype(jnp.bfloat16),
        projections,
        preferred_element_type=jnp.float32,
    ).astype(jnp.bfloat16)
    arrived = lax.all_to_all(outgoing, "img", split_axis=0, concat_axis=0, tiled=True)
    scores = (
        jnp.einsum(
            "rf,jf->rj",
            shifted,
            arrived.reshape(img_count * block_rows, features),
            preferred_element_type=jnp.float32,
        )
        * scale_factor
    )
    scores = scores.reshape(particle_count, shift_count, img_count, block_rows)
    valid_mask = jnp.broadcast_to((live_owner > 0)[None, None, :, None], scores.shape)
    local_top = jnp.max(jnp.where(valid_mask, scores, NEGATIVE), axis=(1, 2, 3))
    local_total = jnp.sum(
        jnp.where(valid_mask, jnp.exp(scores - local_top[:, None, None, None]), 0.0), axis=(1, 2, 3)
    )
    row_top, row_total = merged((local_top, local_total), "ref", merge_pairs)
    evidence = row_top + jnp.log(row_total)
    weights = jnp.where(valid_mask, jnp.exp(scores - evidence[:, None, None, None]), 0.0).astype(
        jnp.bfloat16
    )
    weights = weights.reshape(particle_count * shift_count, img_count * block_rows)
    partial_value = jnp.einsum("rj,rf->jf", weights, shifted, preferred_element_type=jnp.float32)
    partial_value = partial_value.reshape(img_count, block_rows, features)
    returned = lax.all_to_all(partial_value, "img", split_axis=0, concat_axis=0, tiled=True)
    weighted = jnp.einsum(
        "qk,qef->kef", requested.astype(jnp.float32), returned, precision=lax.Precision.HIGHEST
    )
    return (insert_slab(weighted, insertion, VOX), evidence)


def solution(mesh):
    in_specs = (P("img", None), P(("img", "ref"), None, None), P(), P(("img", "ref"), None, None))
    out_specs = (P(None, ("img", "ref")), P("img"))
    return jax.shard_map(
        per_device, mesh=mesh, in_specs=in_specs, out_specs=out_specs, check_vma=False
    )
```

profile of v0, /device:TPU:0, one launch (start us, length us, event | category | flops | bytes accessed | tf_op | source)
XLA Modules:
  0.0 136.5 jit_solution(13730281076805136958)
XLA Ops:
  0.7 0.8 copy.15
  1.6 0.4 convolution_convert_fusion
  1.9 1.1 copy.17
  3.0 7.3 %all-to-all-start = ((bf16[8,8,4096]{2,1,0:T(8,128)(2,1)}), bf16[8,8,4096]{2,1,0:T(8,128)(2,1)S(1)}, u32[]{:S(2)}, u32[]{:S(2)}) async-start(bf16[8,8,4096]{2,1,0:T(8,128)(2,1)} %copy.17), calls=%async_computation | async-start | bytes 1048576 | tf_op jit(solution)/shard_map/all_to_all | solution.py:100
  10.3 0.3 dynamic-slice_reduce_fusion
  10.6 2.1 %slice_convert_fusion.1 = (f32[256,2048]{1,0:T(8,128)S(1)}, f32[256,2048]{1,0:T(8,128)S(1)}) fusion(bf16[256,4096]{1,0:T(8,128)(2,1)} %param.8), kind=kLoop, calls=%fused_computation.18 | loop fusion | flops 1048576 | bytes 6291456 | tf_op jit(solution)/shard_map/convert_element_type | solution.py:35
  12.6 1.0 fusion.17
  13.6 7.7 %add_convert_fusion = (bf16[256,5,2048]{2,1,0:T(8,128)(2,1)}, bf16[256,5,2048]{2,1,0:T(8,128)(2,1)}) fusion(f32[5,2048]{1,0:T(8,128)S(1)} %get-tuple-element.53, f32[256,2048]{1,0:T(8,128)S(1)} %get-tuple-element.49, f32[5,2048]{1,0:T(8,128)S(1)} %get-tuple-element.52, f32[256,2048]{1,0:T(8,128)S(1)} %get-tuple-element.48), kind=kLoop, calls=%fused_computation.3 | loop fusion | flops 20971520 | bytes 14761984 | tf_op jit(solution)/shard_map/convert.3
  21.3 10.0 %sub.60 = bf16[1280,2048]{1,0:T(8,128)(2,1)} reshape(bf16[256,5,2048]{2,1,0:T(8,128)(2,1)} %get-tuple-element.47) | data formatting | bytes 10485760 | tf_op jit(solution)/shard_map/sub | solution.py:37
  31.3 5.8 %constant_dynamic-update-slice_fusion.1 = bf16[1280,4096]{1,0:T(8,128)(2,1)} fusion(bf16[1280,2048]{1,0:T(8,128)(2,1)} %sub.60), kind=kLoop, calls=%fused_computation.54 | loop fusion | bytes 10485760
  37.1 10.1 %add.84 = bf16[1280,2048]{1,0:T(8,128)(2,1)} reshape(bf16[256,5,2048]{2,1,0:T(8,128)(2,1)} %get-tuple-element.46) | data formatting | bytes 10485760 | tf_op jit(solution)/shard_map/add | solution.py:38
  47.2 5.7 %constant_dynamic-update-slice_fusion = bf16[1280,4096]{1,0:T(8,128)(2,1)} fusion(bf16[1280,4096]{1,0:T(8,128)(2,1)} %constant_dynamic-update-slice_fusion.1, bf16[1280,2048]{1,0:T(8,128)(2,1)} %add.84), kind=kLoop, calls=%fused_computation.53 | loop fusion | bytes 10485760 | tf_op jit(solution)/shard_map/concatenate | solution.py:39
  53.2 7.3 %select_reduce_fusion.1 = (f32[1280]{0:T(1024)S(1)}, f32[1280,64]{0,1:T(8,128)S(1)}) fusion(pred[64]{0:T(512)(128)(4,1)S(1)} %broadcast_in_dim.14, bf16[1280,4096]{1,0:T(8,128)(2,1)} %constant_dynamic-update-slice_fusion, bf16[8,8,4096]{2,1,0:T(8,128)(2,1)S(1)} %all-to-all-done), kind=kOutput, calls=%fused_computation.22 | convolution fusion | flops 671333120 | bytes 11342912 | tf_op jit(solution)/shard_map/rf,jf->rj/dot_general | solution.py:102
  61.6 5.1 %all-gather.3 = f32[4,1,256]{2,1,0:T(1,128)S(1)} all-gather(f32[1,1,256]{2,1,0:T(1,128)S(1)} %bitcast.62), channel_id=3, replica_groups=mesh['img'=8,'ref'=4] {'ref'}, dimensions={0}, use_global_device_ids=true | all-gather | bytes 5120 | tf_op jit(solution)/shard_map/all_gather | solution.py:18
  66.7 5.1 %all-gather.2 = f32[4,1,256]{2,1,0:T(1,128)S(1)} all-gather(f32[1,1,256]{2,1,0:T(1,128)S(1)} %bitcast.61), channel_id=2, replica_groups=mesh['img'=8,'ref'=4] {'ref'}, dimensions={0}, use_global_device_ids=true | all-gather | bytes 5120 | tf_op jit(solution)/shard_map/all_gather | solution.py:18
  72.2 6.9 %fusion = f32[8,8,4096]{2,1,0:T(8,128)} fusion(bf16[1280,4096]{1,0:T(8,128)(2,1)} %constant_dynamic-update-slice_fusion, f32[1280,64]{0,1:T(8,128)S(1)} %get-tuple-element.55, f32[1280]{0:T(1024)S(1)} %sub.66, pred[64]{0:T(512)(128)(4,1)S(1)} %broadcast_in_dim.14), kind=kOutput, calls=%fused_computation.5 | convolution fusion | flops 671334400 | bytes 11867200 | tf_op jit(solution)/shard_map/rj,rf->jf/dot_general | solution.py:122
  79.1 6.0 %all-to-all-start.1 = ((f32[8,8,4096]{2,1,0:T(8,128)}), f32[8,8,4096]{2,1,0:T(8,128)S(1)}, u32[]{:S(2)}, u32[]{:S(2)}) async-start(f32[8,8,4096]{2,1,0:T(8,128)} %fusion), calls=%async_computation.1 | async-start | bytes 2097152 | tf_op jit(solution)/shard_map/all_to_all | solution.py:124
  85.1 3.9 %fusion.2 = f32[64,32768]{1,0:T(8,128)} fusion(s32[32768]{0:T(1024)S(1)} %get-tuple-element.51), kind=kLoop, calls=%fused_computation.10 | loop fusion | flops 4194304 | bytes 8519680 | tf_op jit(solution)/shard_map/convert_element_type | solution.py:59
  89.0 22.4 %all-to-all-done.1 = f32[8,8,4096]{2,1,0:T(8,128)S(1)} async-done(((f32[8,8,4096]{2,1,0:T(8,128)}), f32[8,8,4096]{2,1,0:T(8,128)S(1)}, u32[]{:S(2)}, u32[]{:S(2)}) %all-to-all-start.1) | async-done | bytes 1048608 | tf_op jit(solution)/shard_map/all_to_all | solution.py:124
  111.4 1.5 %fusion.5 = f32[2,8,4096]{2,0,1:T(2,128)S(1)} fusion(f32[8,8,4096]{2,1,0:T(8,128)S(1)} %all-to-all-done.1, s32[8,8,4,2]{0,3,2,1:T(2,128)S(1)} %bitcast.56, s32[]{:T(128)S(6)} %select_n.71, s32[]{:T(128)S(6)} %select_n.73), kind=kOutput, calls=%fused_computation.15 | convolution fusion | flops 6291472 | bytes 1311752 | tf_op jit(solution)/shard_map/qk,qef->kef/dot_general | solution.py:125
  113.1 0.2 reshape.268
  113.3 10.8 %broadcast_multiply_fusion = f32[2,64,32768]{2,1,0:T(8,128)} fusion(f32[64,32768]{1,0:T(8,128)} %fusion.2, f32[2,32768]{1,0:T(2,128)S(1)} %bitcast.49), kind=kLoop, calls=%fused_computation.8 | loop fusion | flops 4194304 | bytes 25427968 | tf_op jit(solution)/shard_map/mul | solution.py:68
  124.1 11.8 %fusion.3 = f32[128,64]{1,0:T(8,128)S(1)} fusion(f32[128,32768]{1,0:T(8,128)} %bitcast.48, s32[32768]{0:T(1024)S(1)} %get-tuple-element.50), kind=kOutput, calls=%fused_computation.11 | convolution fusion | flops 3223322624 | bytes 16941056 | tf_op jit(solution)/shard_map/an,bn->ab/dot_general | solution.py:69
  135.8 0.7 reshape.270
  (39 shorter events, 2.2 us)
Async XLA Ops:
  0.6 0.9 copy-start
  3.0 50.2 %all-to-all-start = ((bf16[8,8,4096]{2,1,0:T(8,128)(2,1)}), bf16[8,8,4096]{2,1,0:T(8,128)(2,1)S(1)}, u32[]{:S(2)}, u32[]{:S(2)}) async-start(bf16[8,8,4096]{2,1,0:T(8,128)(2,1)} %copy.17), calls=%async_computation | async-start | bytes 1048576 | tf_op jit(solution)/shard_map/all_to_all | solution.py:100
  37.1 16.0 %copy-start.2 = (s32[2,8,2048]{2,1,0:T(8,128)S(1)}, s32[2,8,2048]{2,1,0:T(8,128)}, u32[]{:S(2)}) copy-start(s32[2,8,2048]{2,1,0:T(8,128)} %param.11) | copy-start | bytes 393220
  71.9 17.2 %copy-start.3 = (f32[256]{0:T(256)}, f32[256]{0:T(256)S(1)}, u32[]{:S(2)}) copy-start(f32[256]{0:T(256)S(1)} %log_add_fusion) | copy-start | bytes 3076
  79.1 32.3 %all-to-all-start.1 = ((f32[8,8,4096]{2,1,0:T(8,128)}), f32[8,8,4096]{2,1,0:T(8,128)S(1)}, u32[]{:S(2)}, u32[]{:S(2)}) async-start(f32[8,8,4096]{2,1,0:T(8,128)} %fusion), calls=%async_computation.1 | async-start | bytes 2097152 | tf_op jit(solution)/shard_map/all_to_all | solution.py:124
  113.3 23.2 %copy-start.1 = (bf16[2,8,4096]{2,1,0:T(8,128)(2,1)S(1)}, bf16[2,8,4096]{2,1,0:T(8,128)(2,1)}, u32[]{:S(2)}) copy-start(bf16[2,8,4096]{2,1,0:T(8,128)(2,1)} %param.9) | copy-start | bytes 393220
where the time goes:
time: 137 us
  local copies, waits for them, and re-layouts  35.9 us (26%)
  matrix products  27.8 us (20%)
  other arithmetic  26.2 us (19%)
  waiting for transfers between devices  22.4 us (16%)
  starting transfers between devices  13.2 us (10%)
  blocking collectives  10.1 us (7%)
    all_to_all x1, waiting for transfers between devices, per_device(): lax.all_to_all(partial_value, 'img', split_axis=0, concat_axis=0, tiled=T...  22.4 us
    dot_general x1, matrix products, insert_slab(): jnp.einsum('an,bn->ab', scaled_rows, low_table, precision=lax.Precision.H...  11.8 us
    mul x1, other arithmetic, insert_slab(): coefficients[:, None, :] * high_table[None, :, :]  10.8 us
    all_gather x2, blocking collectives, merged(): pieces = jax.tree.map(lambda part: lax.all_gather(part, axis), value)  10.1 us
    add x1, local copies, waits for them, and re-layouts, shifted_images(): new_imag = real_part * sine_table + imag_part * cosine  10.1 us
    sub x1, local copies, waits for them, and re-layouts, shifted_images(): new_real = real_part * cosine - imag_part * sine_table  10 us
    another operation x1, other arithmetic  7.69 us
    dot_general x1, matrix products, per_device(): jnp.einsum('rf,jf->rj', shifted, arrived.reshape(img_count * block_rows,...  7.28 us
  transfers between devices with their start and end apart: 2, of which 1 were waited for; matrix products, arithmetic and copies ran while one was open for 34% of the time, Pallas kernels for 0%

commit v1 on v0

v1 whole, which is shorter than its diff:
```python
import math

import jax
import jax.numpy as jnp
import numpy as np
from jax import lax
from jax.experimental import pallas as pl
from jax.experimental.pallas import tpu as pltpu
from jax.sharding import PartitionSpec as P

SIDE = 64
VOX = 4096
LOW = 128
SHIFTS = 5
NEGATIVE = -1e30
ROWS = 16
COLS = 512
VMEM_BYTES = 56 * 1024 * 1024
NT = (((1,), (1,)), ((), ()))
NN = (((1,), (0,)), ((), ()))


def rotation_tables(pixels):
    positions = np.arange(pixels, dtype=np.int64)
    step = np.float32(2.0 * math.pi / SIDE)
    angle_x = (step * (positions % SIDE - SIDE // 2).astype(np.float32)).astype(np.float64)
    angle_y = (step * (positions // SIDE).astype(np.float32)).astype(np.float64)
    table = np.stack([np.cos(angle_x), np.sin(angle_x), np.cos(angle_y), np.sin(angle_y)])
    return np.concatenate([table, np.zeros_like(table)]).astype(np.float32)


def shift_images(part_ref, table_ref, sh_ref):
    particles, features = part_ref.shape
    pixels = features // 2

    @pl.loop(0, particles // ROWS)
    def _(step):
        rows = pl.ds(pl.multiple_of(step * ROWS, ROWS), ROWS)
        for start in range(0, pixels, COLS):
            left = pl.ds(start, COLS)
            right = pl.ds(pixels + start, COLS)
            real16 = part_ref[rows, left]
            imag16 = part_ref[rows, right]
            sh_ref[0, rows, left] = real16
            sh_ref[0, rows, right] = imag16
            real = real16.astype(jnp.float32)
            imag = imag16.astype(jnp.float32)
            for axis in range(2):
                cosine = table_ref[2 * axis : 2 * axis + 1, left]
                sine = table_ref[2 * axis + 1 : 2 * axis + 2, left]
                real_cos, imag_sin = real * cosine, imag * sine
                real_sin, imag_cos = real * sine, imag * cosine
                plus, minus = 1 + 2 * axis, 2 + 2 * axis
                sh_ref[plus, rows, left] = (real_cos - imag_sin).astype(jnp.bfloat16)
                sh_ref[plus, rows, right] = (real_sin + imag_cos).astype(jnp.bfloat16)
                sh_ref[minus, rows, left] = (real_cos + imag_sin).astype(jnp.bfloat16)
                sh_ref[minus, rows, right] = (imag_cos - real_sin).astype(jnp.bfloat16)


def score_images(sh_ref, arrived, live, score_ref):
    scale = 2.0 / math.sqrt(arrived.shape[1])
    top = None
    for t in range(SHIFTS):
        score = scale * lax.dot_general(arrived, sh_ref[t], NT, preferred_element_type=jnp.float32)
        score = jnp.where(live > 0, score, NEGATIVE)
        score_ref[t] = score
        best = jnp.max(score, axis=0, keepdims=True)
        top = best if top is None else jnp.maximum(top, best)
    total = jnp.zeros_like(top)
    for t in range(SHIFTS):
        terms = jnp.where(live > 0, jnp.exp(score_ref[t] - top), 0.0)
        total = total + jnp.sum(terms, axis=0, keepdims=True)
    return top, total


def merge_stats(tops, totals):
    top = tops[0]
    for other in tops[1:]:
        top = jnp.maximum(top, other)
    total = sum(t * jnp.exp(m - top) for m, t in zip(tops, totals))
    return top + jnp.log(total)


def weigh(score_ref, live, evidence):
    return [
        jnp.where(live > 0, jnp.exp(score_ref[t] - evidence), 0.0).astype(jnp.bfloat16)
        for t in range(SHIFTS)
    ]


def insert_row(ids, real, imag):
    count = ids.shape[1]
    highs = VOX // LOW
    high = jnp.right_shift(ids, 7)
    low = jnp.bitwise_and(ids, LOW - 1)
    hit = lax.broadcasted_iota(jnp.int32, (highs, count), 0) == high
    pieces = []
    for value in (real, imag):
        coarse = value.astype(jnp.bfloat16).astype(jnp.float32)
        for piece in (coarse, value - coarse):
            pieces.append(jnp.where(hit, piece, 0.0).astype(jnp.bfloat16))
    table = lax.broadcasted_iota(jnp.int32, (LOW, count), 0) == low
    table = jnp.where(table, 1.0, 0.0).astype(jnp.bfloat16)
    return lax.dot_general(
        jnp.concatenate(pieces, axis=0), table, NT, preferred_element_type=jnp.float32
    )


def score_kernel(part_ref, table_ref, arrived_ref, live_ref, sh_ref, score_ref, stat_ref):
    shift_images(part_ref, table_ref, sh_ref)
    top, total = score_images(sh_ref, arrived_ref[...], live_ref[...], score_ref)
    stat_ref[0:1, :] = top
    stat_ref[1:2, :] = total


def weight_kernel(sh_ref, score_ref, stat_ref, live_ref, partial_ref, evidence_ref):
    count = stat_ref.shape[0]
    evidence = merge_stats(
        [stat_ref[r, 0:1, :] for r in range(count)], [stat_ref[r, 1:2, :] for r in range(count)]
    )
    evidence_ref[...] = evidence
    weights = weigh(score_ref, live_ref[...], evidence)
    features = sh_ref.shape[2]
    for start in range(0, features, 1024):
        columns = pl.ds(start, 1024)
        partial = None
        for t in range(SHIFTS):
            term = lax.dot_general(
                weights[t], sh_ref[t, :, columns], NN, preferred_element_type=jnp.float32
            )
            partial = term if partial is None else partial + term
        partial_ref[:, columns] = partial


def insert_kernel(returned_ref, request_ref, insertion_ref, volume_ref, weighted_ref):
    img_count, block_rows, features = returned_ref.shape
    blocks = insertion_ref.shape[0]
    pixels = features // 2
    highs = VOX // LOW
    for k in range(blocks):

        def add(q, total):
            return total + jnp.where(request_ref[q, k] > 0, returned_ref[q], 0.0)

        weighted_ref[...] = lax.fori_loop(
            0, img_count, add, jnp.zeros((block_rows, features), jnp.float32)
        )
        slab = jnp.zeros((4 * highs, LOW), jnp.float32)
        for e in range(block_rows):
            slab = slab + insert_row(
                insertion_ref[k, e : e + 1, :],
                weighted_ref[e : e + 1, 0:pixels],
                weighted_ref[e : e + 1, pixels:features],
            )
        for c in range(2):
            part = slab[2 * c * highs : (2 * c + 1) * highs]
            part = part + slab[(2 * c + 1) * highs : (2 * c + 2) * highs]
            volume_ref[c] = part if k == 0 else volume_ref[c] + part


VMEM = pl.BlockSpec(memory_space=pltpu.VMEM)
SMEM = pl.BlockSpec(memory_space=pltpu.SMEM)
PARAMS = pltpu.CompilerParams(vmem_limit_bytes=VMEM_BYTES)


def per_device(particles, projections, significance, insertion):
    img_count = lax.axis_size("img")
    ref_count = lax.axis_size("ref")
    img_rank = lax.axis_index("img")
    ref_rank = lax.axis_index("ref")
    blocks_here, block_rows, features = projections.shape
    particle_count = particles.shape[0]
    width = img_count * block_rows
    pattern = significance.reshape(img_count, img_count, ref_count, blocks_here)
    pattern_ref = lax.dynamic_index_in_dim(pattern, ref_rank, 2, keepdims=False)
    wanted = lax.dynamic_index_in_dim(pattern_ref, img_rank, 0, keepdims=False)
    requested = lax.dynamic_index_in_dim(pattern_ref, img_rank, 1, keepdims=False)
    live = jnp.repeat(jnp.sum(wanted, axis=1), block_rows)[:, None]
    outgoing = jnp.zeros((img_count, block_rows, features), jnp.bfloat16)
    for k in range(blocks_here):
        outgoing = jnp.where(requested[:, k][:, None, None] > 0, projections[k][None], outgoing)
    arrived = lax.all_to_all(outgoing, "img", split_axis=0, concat_axis=0, tiled=True)
    table = jnp.asarray(rotation_tables(features // 2))
    shifted, scores, stats = pl.pallas_call(
        score_kernel,
        out_shape=(
            jax.ShapeDtypeStruct((SHIFTS, particle_count, features), jnp.bfloat16),
            jax.ShapeDtypeStruct((SHIFTS, width, particle_count), jnp.float32),
            jax.ShapeDtypeStruct((2, particle_count), jnp.float32),
        ),
        in_specs=[VMEM] * 4,
        out_specs=(VMEM,) * 3,
        compiler_params=PARAMS,
    )(particles, table, arrived.reshape(width, features), live)
    gathered = lax.all_gather(stats, "ref")
    partial, evidence = pl.pallas_call(
        weight_kernel,
        out_shape=(
            jax.ShapeDtypeStruct((width, features), jnp.float32),
            jax.ShapeDtypeStruct((1, particle_count), jnp.float32),
        ),
        in_specs=[VMEM] * 4,
        out_specs=(VMEM,) * 2,
        compiler_params=PARAMS,
    )(shifted, scores, gathered, live)
    returned = lax.all_to_all(
        partial.reshape(img_count, block_rows, features), "img", split_axis=0, concat_axis=0, tiled=True
    )
    volume = pl.pallas_call(
        insert_kernel,
        out_shape=jax.ShapeDtypeStruct((2, VOX // LOW, LOW), jnp.float32),
        in_specs=[VMEM, SMEM, VMEM],
        out_specs=VMEM,
        scratch_shapes=[pltpu.VMEM((block_rows, features), jnp.float32)],
        compiler_params=PARAMS,
    )(returned, requested, insertion)
    return volume.reshape(2, VOX), evidence.reshape(particle_count)


def solution(mesh):
    in_specs = (P("img", None), P(("img", "ref"), None, None), P(), P(("img", "ref"), None, None))
    out_specs = (P(None, ("img", "ref")), P("img"))
    return jax.shard_map(
        per_device, mesh=mesh, in_specs=in_specs, out_specs=out_specs, check_vma=False
    )
```

time: 137 us -> 86.8 us (0.63)
  local copies, waits for them, and re-layouts: 35.9 us -> 6.29 us
  matrix products: 27.8 us -> 0 us
  other arithmetic: 26.2 us -> 1.24 us
  Pallas kernels: 0 us -> 21.6 us
  waiting for transfers between devices: 22.4 us -> 39.1 us
  blocking collectives: 10.1 us -> 6.55 us
  starting transfers between devices: 13.2 us -> 10.9 us
    dot_general x5 -> x0, matrix products: 27.8 us -> none  [the longest x1 11.8 us: insert_slab(): jnp.einsum('an,bn->ab', scaled_rows, low_table, precision=lax.Precision.H...]
    pallas_call x0 -> x3, Pallas kernels: none -> 21.6 us  [the longest x1 7.38 us: per_device(): pl.pallas_call(score_kernel, out_shape=(jax.ShapeDtypeStruct((SHIFTS, par...]
    all_to_all x1, waiting for transfers between devices: 0.01 us -> 13.4 us  [per_device(): lax.all_to_all(outgoing, 'img', split_axis=0, concat_axis=0, tiled=True)]
    mul x1 -> x0, other arithmetic: 10.8 us -> none  [insert_slab(): coefficients[:, None, :] * high_table[None, :, :]]
    sub x5 -> x0, local copies, waits for them, and re-layouts: 10.6 us -> none  [the longest x1 10 us: shifted_images(): new_real = real_part * cosine - imag_part * sine_table]
    add x1 -> x0, local copies, waits for them, and re-layouts: 10.1 us -> none  [shifted_images(): new_imag = real_part * sine_table + imag_part * cosine]
    another operation x1 -> x0, other arithmetic: 7.69 us -> none
    convert_element_type x3 -> x0, other arithmetic: 5.97 us -> none  [the longest x1 3.9 us: insert_slab(): (high_ids[None, :] == jnp.arange(high_count, dtype=jnp.int32)[:, None]).a...]
  transfers between devices with their start and end apart: 2 -> 2, of which waited for: 1 -> 2; matrix products, arithmetic and copies ran while one was open for 34% -> 2% of each run, Pallas kernels for 0% -> 0%
where the time goes in v1:
time: 86.8 us; the launch traced here: 86.3 us
  waiting for transfers between devices  39.1 us (45%)
  Pallas kernels  21.6 us (25%)
  starting transfers between devices  10.9 us (13%)
  blocking collectives  6.55 us (8%)
  local copies, waits for them, and re-layouts  6.29 us (7%)
  other arithmetic  1.24 us (1%)
    all_to_all x1, waiting for transfers between devices, per_device(): lax.all_to_all(partial.reshape(img_count, block_rows, features), 'img', s...  25.7 us
    all_to_all x1, waiting for transfers between devices, per_device(): lax.all_to_all(outgoing, 'img', split_axis=0, concat_axis=0, tiled=True)  13.4 us
    pallas_call x1, Pallas kernels, per_device(): pl.pallas_call(score_kernel, out_shape=(jax.ShapeDtypeStruct((SHIFTS, par...  7.38 us
    all_to_all x1, starting transfers between devices, per_device(): lax.all_to_all(outgoing, 'img', split_axis=0, concat_axis=0, tiled=True)  7.25 us
    pallas_call x1, Pallas kernels, per_device(): pl.pallas_call(insert_kernel, out_shape=jax.ShapeDtypeStruct((2, VOX // L...  7.12 us
    pallas_call x1, Pallas kernels, per_device(): pl.pallas_call(weight_kernel, out_shape=(jax.ShapeDtypeStruct((width, fea...  7.08 us
    all_gather x1, blocking collectives, per_device(): gathered = lax.all_gather(stats, 'ref')  6.55 us
    unnamed x6, local copies, waits for them, and re-layouts  3.96 us
  transfers between devices with their start and end apart: 2, of which 2 were waited for; matrix products, arithmetic and copies ran while one was open for 2% of the time, Pallas kernels for 0%

profile of v1, /device:TPU:0, one launch (start us, length us, event | category | flops | bytes accessed | tf_op | source)
XLA Modules:
  0.0 86.3 jit_solution(8182713754252815633)
XLA Ops:
  0.6 0.8 copy.15
  1.4 0.9 %slice_bitcast_fusion.1 = (bf16[8,4096]{1,0:T(8,128)(2,1)S(1)}, bf16[8,4096]{1,0:T(8,128)(2,1)S(1)}) fusion(bf16[2,8,4096]{2,1,0:T(8,128)(2,1)} %param.6), kind=kLoop, calls=%fused_computation.2 | loop fusion | bytes 262144 | tf_op jit(solution)/shard_map/jit(_where)/broadcast_in_dim | solution.py:181
  2.3 0.9 %select_select_fusion = bf16[8,8,4096]{2,1,0:T(8,128)(2,1)} fusion(pred[8]{0:T(512)(128)(4,1)S(1)} %get-tuple-element.15, pred[8]{0:T(512)(128)(4,1)S(1)} %get-tuple-element.14, bf16[8,4096]{1,0:T(8,128)(2,1)S(1)} %get-tuple-element.13, bf16[8,4096]{1,0:T(8,128)(2,1)S(1)} %get-tuple-element.12), kind=kLoop, calls=%fused_computation | loop fusion | flops 524288 | bytes 655376 | tf_op jit(solution)/shard_map/jit(_where)/select_n | solution.py:181
  3.2 7.3 %all-to-all-start = ((bf16[8,8,4096]{2,1,0:T(8,128)(2,1)}), bf16[8,8,4096]{2,1,0:T(8,128)(2,1)S(1)}, u32[]{:S(2)}, u32[]{:S(2)}) async-start(bf16[8,8,4096]{2,1,0:T(8,128)(2,1)} %select_select_fusion), calls=%async_computation | async-start | bytes 1048576 | tf_op jit(solution)/shard_map/all_to_all | solution.py:182
  10.5 0.3 dynamic-slice_reduce_fusion
  10.8 0.1 broadcast_in_dim.43
  10.9 0.7 broadcast_in_dim_reshape.4.live_ref
  11.6 13.4 %all-to-all-done = bf16[8,8,4096]{2,1,0:T(8,128)(2,1)S(1)} async-done(((bf16[8,8,4096]{2,1,0:T(8,128)(2,1)}), bf16[8,8,4096]{2,1,0:T(8,128)(2,1)S(1)}, u32[]{:S(2)}, u32[]{:S(2)}) %all-to-all-start) | async-done | bytes 524320 | tf_op jit(solution)/shard_map/all_to_all | solution.py:182
  25.0 0.0 copy-start.1
  25.0 0.8 copy-done.1
  25.8 7.4 %shard_map.68 = (bf16[5,256,4096]{2,1,0:T(8,128)(2,1)}, f32[5,64,256]{2,1,0:T(8,128)}, f32[2,256]{1,0:T(2,128)}) custom-call(bf16[256,4096]{1,0:T(8,128)(2,1)} %part_ref.1, f32[8,2048]{1,0:T(8,128)} %constant.72.clone.table_ref, bf16[64,4096]{1,0:T(8,128)(2,1)} %bitcast.19, s32[64,1]{1,0:T(8,128)} %broadcast_in_dim_reshape.4.live_ref), custom_call_target="tpu_custom_call" | custom-call | tf_op jit(solution)/shard_map/pallas_call | solution.py:184
  33.2 6.6 %all-gather.1.stat_ref = f32[4,2,256]{2,1,0:T(2,128)} all-gather(f32[1,2,256]{2,1,0:T(2,128)} %bitcast.25), channel_id=2, replica_groups=mesh['img'=8,'ref'=4] {'ref'}, dimensions={0}, use_global_device_ids=true | all-gather | bytes 10240 | tf_op jit(solution)/shard_map/all_gather | solution.py:195
  39.7 7.1 %shard_map.69 = (f32[64,4096]{1,0:T(8,128)}, f32[1,256]{1,0:T(1,128)}) custom-call(bf16[5,256,4096]{2,1,0:T(8,128)(2,1)} %get-tuple-element.7.sh_ref, f32[5,64,256]{2,1,0:T(8,128)} %get-tuple-element.8.score_ref, f32[4,2,256]{2,1,0:T(2,128)} %all-gather.1.stat_ref, s32[64,1]{1,0:T(8,128)} %broadcast_in_dim_reshape.4.live_ref), custom_call_target="tpu_custom_call" | custom-call | tf_op jit(solution)/shard_map/pallas_call | solution.py:196
  46.8 3.6 %all-to-all-start.1 = ((f32[8,8,4096]{2,1,0:T(8,128)}), f32[8,8,4096]{2,1,0:T(8,128)S(1)}, u32[]{:S(2)}, u32[]{:S(2)}) async-start(f32[8,8,4096]{2,1,0:T(8,128)} %bitcast.20), calls=%async_computation.1 | async-start | bytes 2097152 | tf_op jit(solution)/shard_map/all_to_all | solution.py:206
  50.4 0.7 copy.18.request_ref
  51.1 25.7 %all-to-all-done.1.returned_ref = f32[8,8,4096]{2,1,0:T(8,128)S(1)} async-done(((f32[8,8,4096]{2,1,0:T(8,128)}), f32[8,8,4096]{2,1,0:T(8,128)S(1)}, u32[]{:S(2)}, u32[]{:S(2)}) %all-to-all-start.1) | async-done | bytes 1048608 | tf_op jit(solution)/shard_map/all_to_all | solution.py:206
  76.8 0.0 copy-start
  76.8 1.0 %copy-done = f32[8,8,4096]{2,1,0:T(8,128)} copy-done((f32[8,8,4096]{2,1,0:T(8,128)}, f32[8,8,4096]{2,1,0:T(8,128)S(1)}, u32[]{:S(2)}) %copy-start) | copy-done | bytes 1048600
  77.8 7.1 %shard_map.70 = f32[2,32,128]{2,1,0:T(8,128)} custom-call(f32[8,8,4096]{2,1,0:T(8,128)} %copy-done, s32[8,2]{1,0:T(8,128)} %copy.18.request_ref, s32[2,8,2048]{2,1,0:T(8,128)} %insertion_ref.1), custom_call_target="tpu_custom_call" | custom-call | tf_op jit(solution)/shard_map/pallas_call | solution.py:209
  84.9 1.4 %copy.21 = f32[1,2,32,128]{3,1,2,0:T(2,128)} copy(f32[1,2,32,128]{3,2,1,0:T(8,128)} %bitcast.21) | data formatting | bytes 65536
  (2 shorter events, 0.0 us)
Async XLA Ops:
  3.2 21.7 %all-to-all-start = ((bf16[8,8,4096]{2,1,0:T(8,128)(2,1)}), bf16[8,8,4096]{2,1,0:T(8,128)(2,1)S(1)}, u32[]{:S(2)}, u32[]{:S(2)}) async-start(bf16[8,8,4096]{2,1,0:T(8,128)(2,1)} %select_select_fusion), calls=%async_computation | async-start | bytes 1048576 | tf_op jit(solution)/shard_map/all_to_all | solution.py:182
  25.0 0.8 copy-start.1
  46.8 30.0 %all-to-all-start.1 = ((f32[8,8,4096]{2,1,0:T(8,128)}), f32[8,8,4096]{2,1,0:T(8,128)S(1)}, u32[]{:S(2)}, u32[]{:S(2)}) async-start(f32[8,8,4096]{2,1,0:T(8,128)} %bitcast.20), calls=%async_computation.1 | async-start | bytes 2097152 | tf_op jit(solution)/shard_map/all_to_all | solution.py:206
  76.8 1.0 %copy-start = (f32[8,8,4096]{2,1,0:T(8,128)}, f32[8,8,4096]{2,1,0:T(8,128)S(1)}, u32[]{:S(2)}) copy-start(f32[8,8,4096]{2,1,0:T(8,128)S(1)} %all-to-all-done.1.returned_ref) | copy-start | bytes 3145732

commit v2 on v1

v2 whole, which is shorter than its diff:
```python
import functools
import math

import jax
import jax.numpy as jnp
import numpy as np
from jax import lax
from jax.experimental import pallas as pl
from jax.experimental.pallas import tpu as pltpu
from jax.sharding import PartitionSpec as P

SIDE = 64
VOX = 4096
LOW = 128
SHIFTS = 5
NEGATIVE = -1e30
ROWS = 16
COLS = 512
VMEM_BYTES = 56 * 1024 * 1024
NT = (((1,), (1,)), ((), ()))
NN = (((1,), (0,)), ((), ()))


def rotation_tables(pixels):
    positions = np.arange(pixels, dtype=np.int64)
    step = np.float32(2.0 * math.pi / SIDE)
    angle_x = (step * (positions % SIDE - SIDE // 2).astype(np.float32)).astype(np.float64)
    angle_y = (step * (positions // SIDE).astype(np.float32)).astype(np.float64)
    table = np.stack([np.cos(angle_x), np.sin(angle_x), np.cos(angle_y), np.sin(angle_y)])
    return np.concatenate([table, np.zeros_like(table)]).astype(np.float32)


def shift_images(part_ref, table_ref, sh_ref):
    particles, features = part_ref.shape
    pixels = features // 2

    @pl.loop(0, particles // ROWS)
    def _(step):
        rows = pl.ds(pl.multiple_of(step * ROWS, ROWS), ROWS)
        for start in range(0, pixels, COLS):
            left = pl.ds(start, COLS)
            right = pl.ds(pixels + start, COLS)
            real16 = part_ref[rows, left]
            imag16 = part_ref[rows, right]
            sh_ref[0, rows, left] = real16
            sh_ref[0, rows, right] = imag16
            real = real16.astype(jnp.float32)
            imag = imag16.astype(jnp.float32)
            for axis in range(2):
                cosine = table_ref[2 * axis : 2 * axis + 1, left]
                sine = table_ref[2 * axis + 1 : 2 * axis + 2, left]
                real_cos, imag_sin = real * cosine, imag * sine
                real_sin, imag_cos = real * sine, imag * cosine
                plus, minus = 1 + 2 * axis, 2 + 2 * axis
                sh_ref[plus, rows, left] = (real_cos - imag_sin).astype(jnp.bfloat16)
                sh_ref[plus, rows, right] = (real_sin + imag_cos).astype(jnp.bfloat16)
                sh_ref[minus, rows, left] = (real_cos + imag_sin).astype(jnp.bfloat16)
                sh_ref[minus, rows, right] = (imag_cos - real_sin).astype(jnp.bfloat16)


def score_images(sh_ref, arrived, live, score_ref):
    scale = 2.0 / math.sqrt(arrived.shape[1])
    top = None
    for t in range(SHIFTS):
        score = scale * lax.dot_general(arrived, sh_ref[t], NT, preferred_element_type=jnp.float32)
        score = jnp.where(live > 0, score, NEGATIVE)
        score_ref[t] = score
        best = jnp.max(score, axis=0, keepdims=True)
        top = best if top is None else jnp.maximum(top, best)
    total = jnp.zeros_like(top)
    for t in range(SHIFTS):
        terms = jnp.where(live > 0, jnp.exp(score_ref[t] - top), 0.0)
        total = total + jnp.sum(terms, axis=0, keepdims=True)
    return top, total


def merge_stats(tops, totals):
    top = tops[0]
    for other in tops[1:]:
        top = jnp.maximum(top, other)
    total = sum(t * jnp.exp(m - top) for m, t in zip(tops, totals))
    return top + jnp.log(total)


def weigh(score_ref, live, evidence):
    return [
        jnp.where(live > 0, jnp.exp(score_ref[t] - evidence), 0.0).astype(jnp.bfloat16)
        for t in range(SHIFTS)
    ]


def insert_row(ids, real, imag):
    count = ids.shape[1]
    highs = VOX // LOW
    high = jnp.right_shift(ids, 7)
    low = jnp.bitwise_and(ids, LOW - 1)
    hit = lax.broadcasted_iota(jnp.int32, (highs, count), 0) == high
    pieces = []
    for value in (real, imag):
        coarse = value.astype(jnp.bfloat16).astype(jnp.float32)
        for piece in (coarse, value - coarse):
            pieces.append(jnp.where(hit, piece, 0.0).astype(jnp.bfloat16))
    table = lax.broadcasted_iota(jnp.int32, (LOW, count), 0) == low
    table = jnp.where(table, 1.0, 0.0).astype(jnp.bfloat16)
    return lax.dot_general(
        jnp.concatenate(pieces, axis=0), table, NT, preferred_element_type=jnp.float32
    )


MESH = pl.DeviceIdType.MESH


def step_kernel(
    img_count,
    ref_count,
    sig_ref,
    part_ref,
    table_ref,
    proj_ref,
    ids_ref,
    volume_ref,
    evidence_ref,
    sh_ref,
    out_ref,
    slot_ref,
    arrived_ref,
    live_ref,
    score_ref,
    stat_ref,
    partial_ref,
    return_ref,
    block_send,
    block_recv,
    stat_send,
    stat_recv,
    sum_send,
    sum_recv,
):
    img = lax.axis_index("img")
    ref = lax.axis_index("ref")
    blocks, block_rows, features = proj_ref.shape
    pixels = features // 2
    chunks, _, _, span = partial_ref.shape
    half = span // 2
    particles = part_ref.shape[0]

    barrier = pltpu.get_barrier_semaphore()
    for d in range(1, img_count):
        pl.semaphore_signal(
            barrier, inc=1, device_id={"img": lax.rem(img + d, img_count)}, device_id_type=MESH
        )
    for d in range(1, ref_count):
        pl.semaphore_signal(
            barrier, inc=1, device_id={"ref": lax.rem(ref + d, ref_count)}, device_id_type=MESH
        )

    own = (img * ref_count + ref) * blocks

    def asked(d, k):
        return sig_ref[lax.rem(img + d, img_count), own + k]

    for d in range(img_count):
        chosen = jnp.zeros((block_rows, features), jnp.float32)
        for k in range(blocks):
            chosen = jnp.where(asked(d, k) > 0, proj_ref[k].astype(jnp.float32), chosen)
        chosen = jnp.concatenate([chosen[:, :pixels], chosen[:, pixels:]], axis=0)
        out_ref[d] = chosen.astype(jnp.bfloat16)
    pl.semaphore_wait(barrier, img_count + ref_count - 2)

    block_copies = {}
    for d in range(1, img_count):
        block_copies[d] = pltpu.make_async_remote_copy(
            src_ref=out_ref.at[d],
            dst_ref=slot_ref.at[d],
            send_sem=block_send.at[d],
            recv_sem=block_recv.at[d],
            device_id={"img": lax.rem(img + d, img_count)},
            device_id_type=MESH,
        )
        block_copies[d].start()

    for d in range(img_count):
        alive = jnp.int32(0)
        source = lax.rem(img - d + img_count, img_count)
        for k in range(blocks):
            alive = alive + sig_ref[img, (source * ref_count + ref) * blocks + k]
        live_ref[pl.ds(d * block_rows, block_rows), :] = jnp.full(
            (block_rows, particles), alive.astype(jnp.float32)
        )
    shift_images(part_ref, table_ref, sh_ref)

    slot_ref[0] = out_ref[0]
    for d in range(1, img_count):
        block_copies[d].wait_recv()
    for d in range(0, img_count, 2):
        pair = [slot_ref[d].astype(jnp.float32), slot_ref[d + 1].astype(jnp.float32)]
        for c in range(2):
            rows = jnp.concatenate([p[c * block_rows : (c + 1) * block_rows] for p in pair], axis=0)
            arrived_ref[pl.ds(d * block_rows, 2 * block_rows), pl.ds(c * pixels, pixels)] = rows.astype(
                jnp.bfloat16
            )

    live = live_ref[...]
    top, total = score_images(sh_ref, arrived_ref[...], live, score_ref)
    stat_ref[0] = jnp.zeros_like(stat_ref[0])
    stat_ref[0, 0:1, :] = top
    stat_ref[0, 1:2, :] = total
    stat_copies = []
    for d in range(1, ref_count):
        copy = pltpu.make_async_remote_copy(
            src_ref=stat_ref.at[0],
            dst_ref=stat_ref.at[d],
            send_sem=stat_send.at[d],
            recv_sem=stat_recv.at[d],
            device_id={"ref": lax.rem(ref + d, ref_count)},
            device_id_type=MESH,
        )
        copy.start()
        stat_copies.append(copy)
    for copy in stat_copies:
        copy.wait_recv()
    evidence = merge_stats(
        [stat_ref[r, 0:1, :] for r in range(ref_count)],
        [stat_ref[r, 1:2, :] for r in range(ref_count)],
    )
    evidence_ref[...] = evidence
    weights = weigh(score_ref, live, evidence)

    sum_copies = [[] for _ in range(chunks)]
    for j in range(chunks):
        for c in range(2):
            columns = pl.ds(c * pixels + j * half, half)
            partial = None
            for t in range(SHIFTS):
                term = lax.dot_general(
                    weights[t], sh_ref[t, :, columns], NN, preferred_element_type=jnp.float32
                )
                partial = term if partial is None else partial + term
            for d in range(img_count):
                rows = partial[d * block_rows : (d + 1) * block_rows]
                partial_ref[j, d, :, pl.ds(c * half, half)] = rows
        for d in range(1, img_count):
            copy = pltpu.make_async_remote_copy(
                src_ref=partial_ref.at[j, d],
                dst_ref=return_ref.at[j, d],
                send_sem=sum_send.at[j, d],
                recv_sem=sum_recv.at[j, d],
                device_id={"img": lax.rem(img - d + img_count, img_count)},
                device_id_type=MESH,
            )
            copy.start()
            sum_copies[j].append(copy)

    highs = VOX // LOW
    slab = jnp.zeros((4 * highs, LOW), jnp.float32)
    for j in range(chunks):
        for copy in sum_copies[j]:
            copy.wait_recv()
        for k in range(blocks):
            weighted = jnp.where(asked(0, k) > 0, partial_ref[j, 0], 0.0)
            for d in range(1, img_count):
                weighted = weighted + jnp.where(asked(d, k) > 0, return_ref[j, d], 0.0)
            for e in range(block_rows):
                slab = slab + insert_row(
                    ids_ref[k, e : e + 1, pl.ds(j * half, half)],
                    weighted[e : e + 1, :half],
                    weighted[e : e + 1, half:],
                )
    for c in range(2):
        part = slab[2 * c * highs : (2 * c + 1) * highs]
        volume_ref[c] = part + slab[(2 * c + 1) * highs : (2 * c + 2) * highs]

    for d in range(1, img_count):
        block_copies[d].wait_send()
    for copy in stat_copies:
        copy.wait_send()
    for copies in sum_copies:
        for copy in copies:
            copy.wait_send()


VMEM = pl.BlockSpec(memory_space=pltpu.VMEM)
SMEM = pl.BlockSpec(memory_space=pltpu.SMEM)
CHUNKS = 4


def per_device(particles, projections, significance, insertion):
    img_count = lax.axis_size("img")
    ref_count = lax.axis_size("ref")
    blocks_here, block_rows, features = projections.shape
    particle_count = particles.shape[0]
    width = img_count * block_rows
    pixels = features // 2
    table = jnp.asarray(rotation_tables(pixels))
    volume, evidence = pl.pallas_call(
        functools.partial(step_kernel, img_count, ref_count),
        out_shape=(
            jax.ShapeDtypeStruct((2, VOX // LOW, LOW), jnp.float32),
            jax.ShapeDtypeStruct((1, particle_count), jnp.float32),
        ),
        in_specs=[SMEM] + [VMEM] * 4,
        out_specs=(VMEM,) * 2,
        scratch_shapes=[
            pltpu.VMEM((SHIFTS, particle_count, features), jnp.bfloat16),
            pltpu.VMEM((img_count, 2 * block_rows, pixels), jnp.bfloat16),
            pltpu.VMEM((img_count, 2 * block_rows, pixels), jnp.bfloat16),
            pltpu.VMEM((width, features), jnp.bfloat16),
            pltpu.VMEM((width, particle_count), jnp.float32),
            pltpu.VMEM((SHIFTS, width, particle_count), jnp.float32),
            pltpu.VMEM((ref_count, 8, particle_count), jnp.float32),
            pltpu.VMEM((CHUNKS, img_count, block_rows, features // CHUNKS), jnp.float32),
            pltpu.VMEM((CHUNKS, img_count, block_rows, features // CHUNKS), jnp.float32),
            pltpu.SemaphoreType.DMA((img_count,)),
            pltpu.SemaphoreType.DMA((img_count,)),
            pltpu.SemaphoreType.DMA((ref_count,)),
            pltpu.SemaphoreType.DMA((ref_count,)),
            pltpu.SemaphoreType.DMA((CHUNKS, img_count)),
            pltpu.SemaphoreType.DMA((CHUNKS, img_count)),
        ],
        compiler_params=pltpu.CompilerParams(
            vmem_limit_bytes=VMEM_BYTES, collective_id=0, has_side_effects=True
        ),
    )(significance, particles, table, projections, insertion)
    return volume.reshape(2, VOX), evidence.reshape(particle_count)


def solution(mesh):
    in_specs = (P("img", None), P(("img", "ref"), None, None), P(), P(("img", "ref"), None, None))
    out_specs = (P(None, ("img", "ref")), P("img"))
    return jax.shard_map(
        per_device, mesh=mesh, in_specs=in_specs, out_specs=out_specs, check_vma=False
    )
```

time: 86.8 us -> 58.8 us (0.68)
  waiting for transfers between devices: 39.1 us -> 0 us
  Pallas kernels: 21.6 us -> 55.3 us
  starting transfers between devices: 10.9 us -> 0 us
  blocking collectives: 6.55 us -> 0 us
  local copies, waits for them, and re-layouts: 6.29 us -> 2.63 us
  other arithmetic: 1.24 us -> 0 us
    all_to_all x2 -> x0, waiting for transfers between devices: 39.1 us -> none  [the longest x1 25.7 us: per_device(): lax.all_to_all(partial.reshape(img_count, block_rows, features), 'img', s...]
    pallas_call x3 -> x1, Pallas kernels: 21.6 us -> 55.3 us  [per_device(): pl.pallas_call(functools.partial(step_kernel, img_count, ref_count), out_...]
    all_to_all x2 -> x0, starting transfers between devices: 10.9 us -> none  [the longest x1 7.25 us: per_device(): lax.all_to_all(outgoing, 'img', split_axis=0, concat_axis=0, tiled=True)]
    all_gather x1 -> x0, blocking collectives: 6.55 us -> none  [per_device(): gathered = lax.all_gather(stats, 'ref')]
    unnamed x6 -> x2, local copies, waits for them, and re-layouts: 3.96 us -> 2.63 us
    broadcast_in_dim x2 -> x0, local copies, waits for them, and re-layouts: 0.96 us -> none  [the longest x1 0.88 us: per_device(): jnp.where(requested[:, k][:, None, None] > 0, projections[k][None], outgo...]
    select_n x1 -> x0, other arithmetic: 0.92 us -> none  [per_device(): jnp.where(requested[:, k][:, None, None] > 0, projections[k][None], outgo...]
  transfers between devices with their start and end apart: 2 -> 0, of which waited for: 2 -> 0; matrix products, arithmetic and copies ran while one was open for 2% -> 0% of each run, Pallas kernels for 0% -> 0%
where the time goes in v2:
time: 58.8 us; the launch traced here: 58.6 us
  Pallas kernels  55.3 us (94%)
  local copies, waits for them, and re-layouts  2.63 us (4%)
  between operations  0.64 us (1%)
    pallas_call x1, Pallas kernels, per_device(): pl.pallas_call(functools.partial(step_kernel, img_count, ref_count), out_...  55.3 us
    unnamed x2, local copies, waits for them, and re-layouts  2.63 us

profile of v2, /device:TPU:0, one launch (start us, length us, event | category | flops | bytes accessed | tf_op | source)
XLA Modules:
  0.0 58.6 jit_solution(3331665205381513765)
XLA Ops:
  0.6 55.3 %shard_map.68 = (f32[2,32,128]{2,1,0:T(8,128)}, f32[1,256]{1,0:T(1,128)}) custom-call(s32[8,64]{1,0:T(8,128)} %sig_ref.1, bf16[256,4096]{1,0:T(8,128)(2,1)} %part_ref.1, f32[8,2048]{1,0:T(8,128)} %constant.2.clone.table_ref, bf16[2,8,4096]{2,1,0:T(8,128)(2,1)} %proj_ref.1, s32[2,8,2048]{2,1,0:T(8,128)} %ids_ref.1), custom_call_target="tpu_custom_call" | custom-call | tf_op jit(solution)/shard_map/pallas_call | solution.py:295
  55.9 1.4 %copy.9 = f32[1,2,32,128]{3,1,2,0:T(2,128)} copy(f32[1,2,32,128]{3,2,1,0:T(8,128)} %bitcast.6) | data formatting | bytes 65536
  57.3 1.2 %copy.11 = f32[256]{0:T(256)} copy(f32[256]{0:T(256)} %bitcast.7) | data formatting | bytes 2048

commit v3 on v2

--- a/solution.py
+++ b/solution.py
@@ -129,12 +129,19 @@
     stat_ref,
     partial_ref,
     return_ref,
+    far_ref,
+    joint_ref,
+    joined_ref,
     block_send,
     block_recv,
     stat_send,
     stat_recv,
     sum_send,
     sum_recv,
+    far_send,
+    far_recv,
+    join_send,
+    join_recv,
 ):
     img = lax.axis_index("img")
     ref = lax.axis_index("ref")
@@ -144,11 +151,20 @@
     half = span // 2
     particles = part_ref.shape[0]
 
+    side = img_count // 2
+    place = lax.rem(img, side)
+    base = img - place
+    mirror = lax.rem(img + side, img_count)
+
+    def ahead(d):
+        return lax.rem(base + (d // side) * side, img_count) + lax.rem(place + d % side, side)
+
+    def behind(d):
+        return lax.rem(base + (d // side) * side, img_count) + lax.rem(place - d % side + side, side)
+
     barrier = pltpu.get_barrier_semaphore()
     for d in range(1, img_count):
-        pl.semaphore_signal(
-            barrier, inc=1, device_id={"img": lax.rem(img + d, img_count)}, device_id_type=MESH
-        )
+        pl.semaphore_signal(barrier, inc=1, device_id={"img": ahead(d)}, device_id_type=MESH)
     for d in range(1, ref_count):
         pl.semaphore_signal(
             barrier, inc=1, device_id={"ref": lax.rem(ref + d, ref_count)}, device_id_type=MESH
@@ -157,7 +173,10 @@
     own = (img * ref_count + ref) * blocks
 
     def asked(d, k):
-        return sig_ref[lax.rem(img + d, img_count), own + k]
+        return sig_ref[ahead(d), own + k]
+
+    def asked_mirror(d, k):
+        return sig_ref[ahead(d), (mirror * ref_count + ref) * blocks + k]
 
     for d in range(img_count):
         chosen = jnp.zeros((block_rows, features), jnp.float32)
@@ -174,14 +193,14 @@
             dst_ref=slot_ref.at[d],
             send_sem=block_send.at[d],
             recv_sem=block_recv.at[d],
-            device_id={"img": lax.rem(img + d, img_count)},
+            device_id={"img": ahead(d)},
             device_id_type=MESH,
         )
         block_copies[d].start()
 
     for d in range(img_count):
         alive = jnp.int32(0)
-        source = lax.rem(img - d + img_count, img_count)
+        source = behind(d)
         for k in range(blocks):
             alive = alive + sig_ref[img, (source * ref_count + ref) * blocks + k]
         live_ref[pl.ds(d * block_rows, block_rows), :] = jnp.full(
@@ -227,6 +246,28 @@
     weights = weigh(score_ref, live, evidence)
 
     sum_copies = [[] for _ in range(chunks)]
+    far_copies = [[] for _ in range(chunks)]
+    join_copies = []
+
+    def join(j):
+        for copy in far_copies[j]:
+            copy.wait_recv()
+        for k in range(blocks):
+            joint = jnp.where(asked_mirror(0, k) > 0, partial_ref[j, side], 0.0)
+            for d in range(1, side):
+                joint = joint + jnp.where(asked_mirror(d, k) > 0, far_ref[j, d], 0.0)
+            joint_ref[j, k] = joint
+        copy = pltpu.make_async_remote_copy(
+            src_ref=joint_ref.at[j],
+            dst_ref=joined_ref.at[j],
+            send_sem=join_send.at[j],
+            recv_sem=join_recv.at[j],
+            device_id={"img": mirror},
+            device_id_type=MESH,
+        )
+        copy.start()
+        join_copies.append(copy)
+
     for j in range(chunks):
         for c in range(2):
             columns = pl.ds(c * pixels + j * half, half)
@@ -239,26 +280,41 @@
             for d in range(img_count):
                 rows = partial[d * block_rows : (d + 1) * block_rows]
                 partial_ref[j, d, :, pl.ds(c * half, half)] = rows
-        for d in range(1, img_count):
+        for d in range(1, side):
+            copy = pltpu.make_async_remote_copy(
+                src_ref=partial_ref.at[j, side + d],
+                dst_ref=far_ref.at[j, d],
+                send_sem=far_send.at[j, d],
+                recv_sem=far_recv.at[j, d],
+                device_id={"img": behind(d)},
+                device_id_type=MESH,
+            )
+            copy.start()
+            far_copies[j].append(copy)
+        for d in range(1, side):
             copy = pltpu.make_async_remote_copy(
                 src_ref=partial_ref.at[j, d],
                 dst_ref=return_ref.at[j, d],
                 send_sem=sum_send.at[j, d],
                 recv_sem=sum_recv.at[j, d],
-                device_id={"img": lax.rem(img - d + img_count, img_count)},
+                device_id={"img": behind(d)},
                 device_id_type=MESH,
             )
             copy.start()
             sum_copies[j].append(copy)
+        if j > 0:
+            join(j - 1)
+    join(chunks - 1)
 
     highs = VOX // LOW
     slab = jnp.zeros((4 * highs, LOW), jnp.float32)
     for j in range(chunks):
         for copy in sum_copies[j]:
             copy.wait_recv()
+        join_copies[j].wait_recv()
         for k in range(blocks):
-            weighted = jnp.where(asked(0, k) > 0, partial_ref[j, 0], 0.0)
-            for d in range(1, img_count):
+            weighted = joined_ref[j, k] + jnp.where(asked(0, k) > 0, partial_ref[j, 0], 0.0)
+            for d in range(1, side):
                 weighted = weighted + jnp.where(asked(d, k) > 0, return_ref[j, d], 0.0)
             for e in range(block_rows):
                 slab = slab + insert_row(
@@ -268,13 +324,15 @@
                 )
     for c in range(2):
         part = slab[2 * c * highs : (2 * c + 1) * highs]
-        volume_ref[c] = part + slab[(2 * c + 1) * highs : (2 * c + 2) * highs]
+        part = part + slab[(2 * c + 1) * highs : (2 * c + 2) * highs]
+        for h in range(highs):
+            volume_ref[c : c + 1, h * LOW : (h + 1) * LOW] = part[h : h + 1]
 
     for d in range(1, img_count):
         block_copies[d].wait_send()
     for copy in stat_copies:
         copy.wait_send()
-    for copies in sum_copies:
+    for copies in sum_copies + far_copies + [join_copies]:
         for copy in copies:
             copy.wait_send()
 
@@ -295,7 +353,7 @@
     volume, evidence = pl.pallas_call(
         functools.partial(step_kernel, img_count, ref_count),
         out_shape=(
-            jax.ShapeDtypeStruct((2, VOX // LOW, LOW), jnp.float32),
+            jax.ShapeDtypeStruct((2, VOX), jnp.float32),
             jax.ShapeDtypeStruct((1, particle_count), jnp.float32),
         ),
         in_specs=[SMEM] + [VMEM] * 4,
@@ -309,19 +367,26 @@
             pltpu.VMEM((SHIFTS, width, particle_count), jnp.float32),
             pltpu.VMEM((ref_count, 8, particle_count), jnp.float32),
             pltpu.VMEM((CHUNKS, img_count, block_rows, features // CHUNKS), jnp.float32),
-            pltpu.VMEM((CHUNKS, img_count, block_rows, features // CHUNKS), jnp.float32),
+            pltpu.VMEM((CHUNKS, img_count // 2, block_rows, features // CHUNKS), jnp.float32),
+            pltpu.VMEM((CHUNKS, img_count // 2, block_rows, features // CHUNKS), jnp.float32),
+            pltpu.VMEM((CHUNKS, blocks_here, block_rows, features // CHUNKS), jnp.float32),
+            pltpu.VMEM((CHUNKS, blocks_here, block_rows, features // CHUNKS), jnp.float32),
             pltpu.SemaphoreType.DMA((img_count,)),
             pltpu.SemaphoreType.DMA((img_count,)),
             pltpu.SemaphoreType.DMA((ref_count,)),
             pltpu.SemaphoreType.DMA((ref_count,)),
-            pltpu.SemaphoreType.DMA((CHUNKS, img_count)),
-            pltpu.SemaphoreType.DMA((CHUNKS, img_count)),
+            pltpu.SemaphoreType.DMA((CHUNKS, img_count // 2)),
+            pltpu.SemaphoreType.DMA((CHUNKS, img_count // 2)),
+            pltpu.SemaphoreType.DMA((CHUNKS, img_count // 2)),
+            pltpu.SemaphoreType.DMA((CHUNKS, img_count // 2)),
+            pltpu.SemaphoreType.DMA((CHUNKS,)),
+            pltpu.SemaphoreType.DMA((CHUNKS,)),
         ],
         compiler_params=pltpu.CompilerParams(
             vmem_limit_bytes=VMEM_BYTES, collective_id=0, has_side_effects=True
         ),
     )(significance, particles, table, projections, insertion)
-    return volume.reshape(2, VOX), evidence.reshape(particle_count)
+    return volume, evidence.reshape(particle_count)
 
 
 def solution(mesh):

time: 58.8 us -> 55.3 us (0.940)
  Pallas kernels: 55.3 us -> 51.8 us
    pallas_call x1, Pallas kernels: 55.3 us -> 51.8 us  [per_device(): pl.pallas_call(functools.partial(step_kernel, img_count, ref_count), out_...]
where the time goes in v3:
time: 55.3 us; the launch traced here: 55.1 us
  Pallas kernels  51.8 us (94%)
  local copies, waits for them, and re-layouts  2.6 us (5%)
  between operations  0.64 us (1%)
    pallas_call x1, Pallas kernels, per_device(): pl.pallas_call(functools.partial(step_kernel, img_count, ref_count), out_...  51.8 us
    unnamed x2, local copies, waits for them, and re-layouts  2.6 us

profile of v3, /device:TPU:0, one launch (start us, length us, event | category | flops | bytes accessed | tf_op | source)
XLA Modules:
  0.0 55.1 jit_solution(17270793002755011030)
XLA Ops:
  0.6 51.8 %shard_map.68 = (f32[2,4096]{1,0:T(2,128)}, f32[1,256]{1,0:T(1,128)}) custom-call(s32[8,64]{1,0:T(8,128)} %sig_ref.1, bf16[256,4096]{1,0:T(8,128)(2,1)} %part_ref.1, f32[8,2048]{1,0:T(8,128)} %constant.2.clone.table_ref, bf16[2,8,4096]{2,1,0:T(8,128)(2,1)} %proj_ref.1, s32[2,8,2048]{2,1,0:T(8,128)} %ids_ref.1), custom_call_target="tpu_custom_call" | custom-call | tf_op jit(solution)/shard_map/pallas_call | solution.py:353
  52.5 1.4 %copy.9 = f32[2,4096]{1,0:T(2,128)} copy(f32[2,4096]{1,0:T(2,128)} %get-tuple-element.8) | data formatting | bytes 65536
  53.8 1.2 %copy.10 = f32[256]{0:T(256)} copy(f32[256]{0:T(256)} %bitcast.1) | data formatting | bytes 2048

commit v4 on v3

--- a/solution.py
+++ b/solution.py
@@ -89,19 +89,22 @@
     ]
 
 
-def insert_row(ids, real, imag):
+def low_table(ids):
+    low = jnp.bitwise_and(ids, LOW - 1)
+    hit = lax.broadcasted_iota(jnp.int32, (LOW, ids.shape[1]), 0) == low
+    return jnp.where(hit, 1.0, 0.0).astype(jnp.bfloat16)
+
+
+def insert_row(ids, table, real, imag):
     count = ids.shape[1]
     highs = VOX // LOW
     high = jnp.right_shift(ids, 7)
-    low = jnp.bitwise_and(ids, LOW - 1)
     hit = lax.broadcasted_iota(jnp.int32, (highs, count), 0) == high
     pieces = []
     for value in (real, imag):
         coarse = value.astype(jnp.bfloat16).astype(jnp.float32)
         for piece in (coarse, value - coarse):
             pieces.append(jnp.where(hit, piece, 0.0).astype(jnp.bfloat16))
-    table = lax.broadcasted_iota(jnp.int32, (LOW, count), 0) == low
-    table = jnp.where(table, 1.0, 0.0).astype(jnp.bfloat16)
     return lax.dot_general(
         jnp.concatenate(pieces, axis=0), table, NT, preferred_element_type=jnp.float32
     )
@@ -132,6 +135,7 @@
     far_ref,
     joint_ref,
     joined_ref,
+    low_ref,
     block_send,
     block_recv,
     stat_send,
@@ -207,6 +211,12 @@
             (block_rows, particles), alive.astype(jnp.float32)
         )
     shift_images(part_ref, table_ref, sh_ref)
+    held = low_ref.shape[2] == pixels
+    for k in range(blocks if held else 0):
+        for e in range(block_rows):
+            for j in range(chunks):
+                columns = pl.ds(j * half, half)
+                low_ref[k * block_rows + e, :, columns] = low_table(ids_ref[k, e : e + 1, columns])
 
     slot_ref[0] = out_ref[0]
     for d in range(1, img_count):
@@ -317,8 +327,10 @@
             for d in range(1, side):
                 weighted = weighted + jnp.where(asked(d, k) > 0, return_ref[j, d], 0.0)
             for e in range(block_rows):
+                ids = ids_ref[k, e : e + 1, pl.ds(j * half, half)]
                 slab = slab + insert_row(
-                    ids_ref[k, e : e + 1, pl.ds(j * half, half)],
+                    ids,
+                    low_ref[k * block_rows + e, :, pl.ds(j * half, half)] if held else low_table(ids),
                     weighted[e : e + 1, :half],
                     weighted[e : e + 1, half:],
                 )
@@ -371,6 +383,7 @@
             pltpu.VMEM((CHUNKS, img_count // 2, block_rows, features // CHUNKS), jnp.float32),
             pltpu.VMEM((CHUNKS, blocks_here, block_rows, features // CHUNKS), jnp.float32),
             pltpu.VMEM((CHUNKS, blocks_here, block_rows, features // CHUNKS), jnp.float32),
+            pltpu.VMEM((blocks_here * block_rows, LOW, pixels if width <= 128 else LOW), jnp.bfloat16),
             pltpu.SemaphoreType.DMA((img_count,)),
             pltpu.SemaphoreType.DMA((img_count,)),
             pltpu.SemaphoreType.DMA((ref_count,)),

time: 55.3 us -> 55.5 us (level)
  no operation moved by 1% of the time
where the time goes in v4:
time: 55.5 us; the launch traced here: 55.2 us
  Pallas kernels  52 us (94%)
  local copies, waits for them, and re-layouts  2.6 us (5%)
  between operations  0.64 us (1%)
    pallas_call x1, Pallas kernels, per_device(): pl.pallas_call(functools.partial(step_kernel, img_count, ref_count), out_...  52 us
    unnamed x2, local copies, waits for them, and re-layouts  2.6 us

profile of v4, /device:TPU:0, one launch (start us, length us, event | category | flops | bytes accessed | tf_op | source)
XLA Modules:
  0.0 55.2 jit_solution(10663326437926256041)
XLA Ops:
  0.6 52.0 %shard_map.68 = (f32[2,4096]{1,0:T(2,128)}, f32[1,256]{1,0:T(1,128)}) custom-call(s32[8,64]{1,0:T(8,128)} %sig_ref.1, bf16[256,4096]{1,0:T(8,128)(2,1)} %part_ref.1, f32[8,2048]{1,0:T(8,128)} %constant.2.clone.table_ref, bf16[2,8,4096]{2,1,0:T(8,128)(2,1)} %proj_ref.1, s32[2,8,2048]{2,1,0:T(8,128)} %ids_ref.1), custom_call_target="tpu_custom_call" | custom-call | tf_op jit(solution)/shard_map/pallas_call | solution.py:365
  52.6 1.4 %copy.9 = f32[2,4096]{1,0:T(2,128)} copy(f32[2,4096]{1,0:T(2,128)} %get-tuple-element.8) | data formatting | bytes 65536
  54.0 1.2 %copy.10 = f32[256]{0:T(256)} copy(f32[256]{0:T(256)} %bitcast.1) | data formatting | bytes 2048

commit v5 on v4

--- a/solution.py
+++ b/solution.py
@@ -30,11 +30,10 @@
     return np.concatenate([table, np.zeros_like(table)]).astype(np.float32)
 
 
-def shift_images(part_ref, table_ref, sh_ref):
-    particles, features = part_ref.shape
-    pixels = features // 2
-
-    @pl.loop(0, particles // ROWS)
+def shift_images(part_ref, table_ref, sh_ref, first, last):
+    pixels = part_ref.shape[1] // 2
+
+    @pl.loop(first // ROWS, last // ROWS)
     def _(step):
         rows = pl.ds(pl.multiple_of(step * ROWS, ROWS), ROWS)
         for start in range(0, pixels, COLS):
@@ -136,6 +135,8 @@
     joint_ref,
     joined_ref,
     low_ref,
+    pack_ref,
+    pair_ref,
     block_send,
     block_recv,
     stat_send,
@@ -182,25 +183,37 @@
     def asked_mirror(d, k):
         return sig_ref[ahead(d), (mirror * ref_count + ref) * blocks + k]
 
-    for d in range(img_count):
-        chosen = jnp.zeros((block_rows, features), jnp.float32)
+    for k in range(blocks):
+        whole = proj_ref[k].astype(jnp.float32)
+        whole = jnp.concatenate([whole[:, :pixels], whole[:, pixels:]], axis=0)
+        pack_ref[k] = whole.astype(jnp.bfloat16)
+
+    def choose(d, source_ref, wanted):
+        chosen = jnp.zeros(source_ref.shape[1:], jnp.float32)
         for k in range(blocks):
-            chosen = jnp.where(asked(d, k) > 0, proj_ref[k].astype(jnp.float32), chosen)
-        chosen = jnp.concatenate([chosen[:, :pixels], chosen[:, pixels:]], axis=0)
-        out_ref[d] = chosen.astype(jnp.bfloat16)
+            chosen = jnp.where(wanted(d, k) > 0, source_ref[k].astype(jnp.float32), chosen)
+        return chosen.astype(jnp.bfloat16)
+
+    for d in range(1, side):
+        out_ref[d] = choose(d, pack_ref, asked)
     pl.semaphore_wait(barrier, img_count + ref_count - 2)
 
     block_copies = {}
-    for d in range(1, img_count):
+
+    def send_block(d, source, target, device):
         block_copies[d] = pltpu.make_async_remote_copy(
-            src_ref=out_ref.at[d],
-            dst_ref=slot_ref.at[d],
+            src_ref=source,
+            dst_ref=target,
             send_sem=block_send.at[d],
             recv_sem=block_recv.at[d],
-            device_id={"img": ahead(d)},
+            device_id={"img": device},
             device_id_type=MESH,
         )
         block_copies[d].start()
+
+    send_block(side, pack_ref, pair_ref, mirror)
+    for d in range(1, side):
+        send_block(d, out_ref.at[d], slot_ref.at[d], ahead(d))
 
     for d in range(img_count):
         alive = jnp.int32(0)
@@ -210,7 +223,14 @@
         live_ref[pl.ds(d * block_rows, block_rows), :] = jnp.full(
             (block_rows, particles), alive.astype(jnp.float32)
         )
-    shift_images(part_ref, table_ref, sh_ref)
+    slot_ref[0] = choose(0, pack_ref, asked)
+    shift_images(part_ref, table_ref, sh_ref, 0, particles // 2)
+    block_copies[side].wait_recv()
+    for d in range(1, side):
+        out_ref[side + d] = choose(d, pair_ref, asked_mirror)
+        send_block(side + d, out_ref.at[side + d], slot_ref.at[side + d], ahead(d))
+    slot_ref[side] = choose(0, pair_ref, asked_mirror)
+    shift_images(part_ref, table_ref, sh_ref, particles // 2, particles)
     held = low_ref.shape[2] == pixels
     for k in range(blocks if held else 0):
         for e in range(block_rows):
@@ -218,9 +238,9 @@
                 columns = pl.ds(j * half, half)
                 low_ref[k * block_rows + e, :, columns] = low_table(ids_ref[k, e : e + 1, columns])
 
-    slot_ref[0] = out_ref[0]
     for d in range(1, img_count):
-        block_copies[d].wait_recv()
+        if d != side:
+            block_copies[d].wait_recv()
     for d in range(0, img_count, 2):
         pair = [slot_ref[d].astype(jnp.float32), slot_ref[d + 1].astype(jnp.float32)]
         for c in range(2):
@@ -384,6 +404,8 @@
             pltpu.VMEM((CHUNKS, blocks_here, block_rows, features // CHUNKS), jnp.float32),
             pltpu.VMEM((CHUNKS, blocks_here, block_rows, features // CHUNKS), jnp.float32),
             pltpu.VMEM((blocks_here * block_rows, LOW, pixels if width <= 128 else LOW), jnp.bfloat16),
+            pltpu.VMEM((blocks_here, 2 * block_rows, pixels), jnp.bfloat16),
+            pltpu.VMEM((blocks_here, 2 * block_rows, pixels), jnp.bfloat16),
             pltpu.SemaphoreType.DMA((img_count,)),
             pltpu.SemaphoreType.DMA((img_count,)),
             pltpu.SemaphoreType.DMA((ref_count,)),

time: 55.5 us -> 55.7 us (level)
  no operation moved by 1% of the time
where the time goes in v5:
time: 55.7 us; the launch traced here: 55.5 us
  Pallas kernels  52.2 us (94%)
  local copies, waits for them, and re-layouts  2.6 us (5%)
  between operations  0.64 us (1%)
    pallas_call x1, Pallas kernels, per_device(): pl.pallas_call(functools.partial(step_kernel, img_count, ref_count), out_...  52.2 us
    unnamed x2, local copies, waits for them, and re-layouts  2.6 us

profile of v5, /device:TPU:0, one launch (start us, length us, event | category | flops | bytes accessed | tf_op | source)
XLA Modules:
  0.0 55.5 jit_solution(12569269946694951772)
XLA Ops:
  0.6 52.2 %shard_map.68 = (f32[2,4096]{1,0:T(2,128)}, f32[1,256]{1,0:T(1,128)}) custom-call(s32[8,64]{1,0:T(8,128)} %sig_ref.1, bf16[256,4096]{1,0:T(8,128)(2,1)} %part_ref.1, f32[8,2048]{1,0:T(8,128)} %constant.2.clone.table_ref, bf16[2,8,4096]{2,1,0:T(8,128)(2,1)} %proj_ref.1, s32[2,8,2048]{2,1,0:T(8,128)} %ids_ref.1), custom_call_target="tpu_custom_call" | custom-call | tf_op jit(solution)/shard_map/pallas_call | solution.py:385
  52.9 1.4 %copy.9 = f32[2,4096]{1,0:T(2,128)} copy(f32[2,4096]{1,0:T(2,128)} %get-tuple-element.8) | data formatting | bytes 65536
  54.3 1.2 %copy.10 = f32[256]{0:T(256)} copy(f32[256]{0:T(256)} %bitcast.1) | data formatting | bytes 2048
